TPU v7x, 32 devices: a whole 2x2x4 slice. The times are simulated.
32 devices in a mesh: pipe: 16 (over z, y, x), tp: 2 (over core).
Axes of the slice: x: 2, y: 2, z: 4, core: 2. Of those that a mesh axis runs over, the one named last changes fastest.
Arguments:
- hidden: bfloat16 [2, 64, 8192], P(None, None, 'tp'), may hold values from -6 to 6
- rewards: float32 [2, 64], replicated, may hold values from -6 to 6
- counts: int32 [2], replicated, may hold values from 1 to 64, as said below
- episode: int32 [2, 64], replicated, may hold values from 0 to 3, as said below
- down_weight: bfloat16 [16, 8192, 256], P('pipe', 'tp'), may hold values from -0.0625 to 0.0625
- up_weight: bfloat16 [16, 256, 8192], P('pipe', None, 'tp'), may hold values from -0.09375 to 0.09375
- head_weight: bfloat16 [8192], P('tp'), may hold values from -0.03125 to 0.03125
Outputs:
- grad_down: float32 [16, 8192, 256], P('pipe', 'tp')
- grad_up: float32 [16, 256, 8192], P('pipe', None, 'tp')
- grad_head: float32 [2, 4096], P('tp', 'pipe')
- advantages: float32 [2, 64], replicated
Inputs may be any that keep to these rules, and one draw needn't show every extreme that they name: Micro-batch m has counts[m] live tokens in its first slots; one micro-batch is full. `episode`: episode ids never fall along a micro-batch; each of the four ids holds 1 to 32 slots of every micro-batch, one of them exactly 32.
All inputs are finite; a program needn't handle non-finite values.
Results may differ from a plain program's by a relative error of at most 0.023.
Values may be sent and summed in bfloat16 or wider, within the bound.
A program may use at most 64 MiB of HBM per device.

v0:
```python
import jax
import jax.numpy as jnp
from jax import lax
from jax.sharding import PartitionSpec as P

DISCOUNT = 1.0
TRACE = 1.0


def shifted(value, axis, steps):
    count = lax.axis_size(axis)
    leading, last = (max(0, -steps), min(count, count - steps))
    return lax.ppermute(value, axis, [(source, source + steps) for source in range(leading, last)])


def derivative(pre_act):
    sigmoid_value = jax.nn.sigmoid(pre_act)
    return sigmoid_value * (1.0 + pre_act * (1.0 - sigmoid_value))


def advantage(values, rewards, counts, episode):
    batch_total = values.shape[0]
    slot_total = values.shape[1]
    position = jnp.arange(slot_total, dtype=jnp.int32)
    live_mask = (position[None, :] < counts[:, None]).astype(jnp.float32)
    next_live = position[None, :] + 1 < counts[:, None]
    same_next = jnp.concatenate(
        [episode[:, 1:] == episode[:, :-1], jnp.zeros((batch_total, 1), jnp.bool_)], axis=1
    )
    follow = (next_live & same_next).astype(jnp.float32)
    next_value = jnp.concatenate([values[:, 1:], jnp.zeros((batch_total, 1), jnp.float32)], axis=1)
    deltas = (rewards + DISCOUNT * follow * next_value - values) * live_mask
    later_mask = position[None, :] >= position[:, None]
    distance = jnp.maximum(position[None, :] - position[:, None], 0).astype(jnp.float32)
    decay_table = jnp.power(jnp.float32(TRACE * DISCOUNT), distance)
    same_episode = episode[:, :, None] == episode[:, None, :]
    weights = jnp.where(
        later_mask[None] & same_episode & (live_mask[:, None, :] > 0),
        decay_table[None],
        jnp.float32(0.0),
    )
    return jnp.einsum("mtk,mk->mt", weights, deltas, precision=lax.Precision.HIGHEST) * live_mask


def place_row(stack, index_value, new_value, active):
    previous = lax.dynamic_index_in_dim(stack, index_value, 0, keepdims=False)
    return lax.dynamic_update_index_in_dim(
        stack, jnp.where(active, new_value, previous), index_value, 0
    )


def local(hidden, rewards, counts, episode, down_weight, up_weight, head_weight):
    section_index = lax.axis_index("pipe")
    section_count = lax.axis_size("pipe")
    tp_count = lax.axis_size("tp")
    down_local = down_weight[0]
    up_local = up_weight[0]
    batch_count, slot_count, local_width = hidden.shape
    inner_width = down_local.shape[1]
    row_count = batch_count * slot_count // batch_count
    tick_count = section_count + batch_count - 1
    kept_width = inner_width // tp_count
    last_section = section_count - 1
    is_last = section_index == last_section

    def forward_act(block_rows):
        partial_sum = jnp.dot(block_rows, down_local, preferred_element_type=jnp.float32)
        pre_act = lax.psum_scatter(partial_sum, "tp", scatter_dimension=1, tiled=True)
        activated = lax.all_gather(
            jax.nn.silu(pre_act).astype(jnp.bfloat16), "tp", axis=1, tiled=True
        )
        return (pre_act, activated)

    def backward_act(grad_out, pre_act):
        partial_sum = jnp.einsum(
            "rd,kd->rk", grad_out, up_local, preferred_element_type=jnp.float32
        )
        share_sum = lax.psum_scatter(partial_sum, "tp", scatter_dimension=1, tiled=True)
        return lax.all_gather(
            (share_sum * derivative(pre_act)).astype(jnp.bfloat16), "tp", axis=1, tiled=True
        )

    def forward_tick(tick_index, state_tuple):
        carried, inputs_kept, pre_kept, act_kept, finals = state_tuple
        group_index = tick_index - section_index
        active = (group_index >= 0) & (group_index < batch_count)
        slot_index = jnp.clip(group_index, 0, batch_count - 1)
        first_rows = lax.dynamic_index_in_dim(
            hidden, jnp.clip(tick_index, 0, batch_count - 1), 0, keepdims=False
        )
        block_rows = jnp.where(section_index == 0, first_rows, carried)
        pre_act, activated = forward_act(block_rows)
        output = (
            block_rows.astype(jnp.float32)
            + jnp.dot(activated, up_local, preferred_element_type=jnp.float32)
        ).astype(jnp.bfloat16)
        inputs_kept = place_row(inputs_kept, slot_index, block_rows, active)
        pre_kept = place_row(pre_kept, slot_index, pre_act, active)
        act_kept = place_row(act_kept, slot_index, activated, active)
        finals = place_row(finals, slot_index, output, active & is_last)
        carried = shifted(output, "pipe", 1)
        return (carried, inputs_kept, pre_kept, act_kept, finals)

    start_state = (
        jnp.zeros((row_count, local_width), jnp.bfloat16),
        jnp.zeros((batch_count, row_count, local_width), jnp.bfloat16),
        jnp.zeros((batch_count, row_count, kept_width), jnp.float32),
        jnp.zeros((batch_count, row_count, inner_width), jnp.bfloat16),
        jnp.zeros((batch_count, row_count, local_width), jnp.bfloat16),
    )
    unused_rows, inputs_kept, pre_kept, act_kept, finals = lax.fori_loop(
        0, tick_count, forward_tick, start_state
    )
    value_part = jnp.einsum("mcd,d->mc", finals, head_weight, preferred_element_type=jnp.float32)
    value_part = jnp.where(is_last, value_part, jnp.zeros_like(value_part))
    values = lax.psum(value_part, ("pipe", "tp"))
    advantages = advantage(values, rewards, counts, episode)
    value_grad = -advantages
    head_part = jnp.einsum(
        "mcd,mc->d", finals.astype(jnp.float32), value_grad, precision=lax.Precision.HIGHEST
    )
    head_part = jnp.where(is_last, head_part, jnp.zeros_like(head_part))
    grad_head = lax.psum_scatter(head_part, "pipe", scatter_dimension=0, tiled=True)
    grad_final = (value_grad[:, :, None] * head_weight.astype(jnp.float32)[None, None, :]).astype(
        jnp.bfloat16
    )

    def backward_tick(tick_index, state_tuple):
        carried, grads_kept, outgrad_kept = state_tuple
        group_index = tick_index - (last_section - section_index)
        active = (group_index >= 0) & (group_index < batch_count)
        slot_index = jnp.clip(group_index, 0, batch_count - 1)
        last_rows = lax.dynamic_index_in_dim(
            grad_final, jnp.clip(tick_index, 0, batch_count - 1), 0, keepdims=False
        )
        grad_out = jnp.where(is_last, last_rows, carried)
        pre_act = lax.dynamic_index_in_dim(pre_kept, slot_index, 0, keepdims=False)
        pre_grad = backward_act(grad_out, pre_act)
        grad_in = (
            grad_out.astype(jnp.float32)
            + jnp.einsum("rk,dk->rd", pre_grad, down_local, preferred_element_type=jnp.float32)
        ).astype(jnp.bfloat16)
        grads_kept = place_row(grads_kept, slot_index, pre_grad, active)
        outgrad_kept = place_row(outgrad_kept, slot_index, grad_out, active)
        carried = shifted(grad_in, "pipe", -1)
        return (carried, grads_kept, outgrad_kept)

    back_state = (
        jnp.zeros((row_count, local_width), jnp.bfloat16),
        jnp.zeros((batch_count, row_count, inner_width), jnp.bfloat16),
        jnp.zeros((batch_count, row_count, local_width), jnp.bfloat16),
    )
    unused_grad, grads_kept, outgrad_kept = lax.fori_loop(0, tick_count, backward_tick, back_state)
    grad_down = jnp.einsum(
        "nd,nk->dk",
        inputs_kept.reshape(-1, local_width),
        grads_kept.reshape(-1, inner_width),
        preferred_element_type=jnp.float32,
    )
    grad_up = jnp.einsum(
        "nk,nd->kd",
        act_kept.reshape(-1, inner_width),
        outgrad_kept.reshape(-1, local_width),
        preferred_element_type=jnp.float32,
    )
    return (grad_down[None], grad_up[None], grad_head[None], advantages)


def solution(mesh):
    return jax.shard_map(
        local,
        mesh=mesh,
        in_specs=(
            P(None, None, "tp"),
            P(),
            P(),
            P(),
            P("pipe", "tp", None),
            P("pipe", None, "tp"),
            P("tp"),
        ),
        out_specs=(P("pipe", "tp", None), P("pipe", None, "tp"), P("tp", "pipe"), P()),
        check_vma=False,
    )
```

profile of v0, /device:TPU:1, one launch (start us, length us, event | category | flops | bytes accessed | tf_op | source)
XLA Modules:
  0.0 1327.8 jit_solution(492986380814527737)
XLA Ops:
  14.5 588.2 %while.41 = (s32[]{:T(128)}, bf16[64,4096]{1,0:T(8,128)(2,1)S(1)}, bf16[2,64,4096]{2,1,0:T(8,128)(2,1)}, f32[2,64,128]{2,1,0:T(8,128)S(1)}, bf16[2,64,256]{2,1,0...) while((s32[]{:T(128)}, bf16[64,4096]{1,0:T(8,128)(2,1)S(1)}, ...), condition=%wide.region_2.3_spmd, body=%wide.region_0.2_spmd.sunk | while | flops 270073856 | bytes 14582645 | solution.py:111
  245.6 11.0 collective-permute-done
  314.8 11.0 collective-permute-done
  604.4 41.7 %psum.7 = f32[2,64]{1,0:T(2,128)S(1)} all-reduce(f32[2,64]{1,0:T(2,128)S(1)} %broadcast_select_fusion.1), channel_id=1, replica_groups=mesh['pipe'=16,'tp'=2] {'pipe','tp'}, use_global_device_ids=true, to_apply=%region_3.4 | all-reduce | flops 128 | bytes 1024 | tf_op jit(solution)/shard_map/psum | solution.py:116
  648.9 61.8 %all-reduce.2 = f32[4096]{0:T(1024)S(1)} all-reduce(f32[4096]{0:T(1024)S(1)} %broadcast_select_fusion), channel_id=4, replica_groups=mesh['pipe'=16,'tp'=2] {'pipe'}, use_global_device_ids=true, to_apply=%region_7.8.clone | all-reduce | flops 4096 | bytes 32768
  713.6 599.4 %while.42 = (s32[]{:T(128)}, bf16[64,4096]{1,0:T(8,128)(2,1)S(1)}, bf16[2,64,256]{2,1,0:T(8,128)(2,1)S(1)}, bf16[2,64,4096]{2,1,0:T(8,128)(2,1)}, pred[]{:T(512)...) while((s32[]{:T(128)}, bf16[64,4096]{1,0:T(8,128)(2,1)S(1)}, ...), condition=%wide.region_6.7_spmd, body=%wide.region_4.6_spmd.sunk | while | flops 269836288 | bytes 20611924 | solution.py:153
  718.4 18.4 %reduce-scatter.5.cloned.1.call-done = f32[64,128]{1,0:T(8,128)} async-done(((f32[64,256]{1,0:T(8,128)}), f32[64,128]{1,0:T(8,128)}) %reduce-scatter.5.cloned.1.call-update) | async-done | bytes 32784 | tf_op jit(solution)/shard_map/while/body/eval_jaxpr/reduce_scatter | solution.py:78
  742.3 14.2 %collective-permute-done.1 = bf16[64,4096]{1,0:T(8,128)(2,1)S(1)} collective-permute-done((bf16[64,4096]{1,0:T(8,128)(2,1)}, bf16[64,4096]{1,0:T(8,128)(2,1)S(1)}, u32[]{:S(2)}, u32[]{:S(2)}) %collective-permute-start.1) | collective-permute-done | bytes 524320 | tf_op jit(solution)/shard_map/while/body/eval_jaxpr/ppermute | solution.py:13
  777.1 14.2 %collective-permute-done.1 = bf16[64,4096]{1,0:T(8,128)(2,1)S(1)} collective-permute-done((bf16[64,4096]{1,0:T(8,128)(2,1)}, bf16[64,4096]{1,0:T(8,128)(2,1)S(1)}, u32[]{:S(2)}, u32[]{:S(2)}) %collective-permute-start.1) | collective-permute-done | bytes 524320 | tf_op jit(solution)/shard_map/while/body/eval_jaxpr/ppermute | solution.py:13
  811.9 14.2 %collective-permute-done.1 = bf16[64,4096]{1,0:T(8,128)(2,1)S(1)} collective-permute-done((bf16[64,4096]{1,0:T(8,128)(2,1)}, bf16[64,4096]{1,0:T(8,128)(2,1)S(1)}, u32[]{:S(2)}, u32[]{:S(2)}) %collective-permute-start.1) | collective-permute-done | bytes 524320 | tf_op jit(solution)/shard_map/while/body/eval_jaxpr/ppermute | solution.py:13
  846.7 14.2 %collective-permute-done.1 = bf16[64,4096]{1,0:T(8,128)(2,1)S(1)} collective-permute-done((bf16[64,4096]{1,0:T(8,128)(2,1)}, bf16[64,4096]{1,0:T(8,128)(2,1)S(1)}, u32[]{:S(2)}, u32[]{:S(2)}) %collective-permute-start.1) | collective-permute-done | bytes 524320 | tf_op jit(solution)/shard_map/while/body/eval_jaxpr/ppermute | solution.py:13
  881.5 14.2 %collective-permute-done.1 = bf16[64,4096]{1,0:T(8,128)(2,1)S(1)} collective-permute-done((bf16[64,4096]{1,0:T(8,128)(2,1)}, bf16[64,4096]{1,0:T(8,128)(2,1)S(1)}, u32[]{:S(2)}, u32[]{:S(2)}) %collective-permute-start.1) | collective-permute-done | bytes 524320 | tf_op jit(solution)/shard_map/while/body/eval_jaxpr/ppermute | solution.py:13
  916.2 14.2 %collective-permute-done.1 = bf16[64,4096]{1,0:T(8,128)(2,1)S(1)} collective-permute-done((bf16[64,4096]{1,0:T(8,128)(2,1)}, bf16[64,4096]{1,0:T(8,128)(2,1)S(1)}, u32[]{:S(2)}, u32[]{:S(2)}) %collective-permute-start.1) | collective-permute-done | bytes 524320 | tf_op jit(solution)/shard_map/while/body/eval_jaxpr/ppermute | solution.py:13
  951.0 14.2 %collective-permute-done.1 = bf16[64,4096]{1,0:T(8,128)(2,1)S(1)} collective-permute-done((bf16[64,4096]{1,0:T(8,128)(2,1)}, bf16[64,4096]{1,0:T(8,128)(2,1)S(1)}, u32[]{:S(2)}, u32[]{:S(2)}) %collective-permute-start.1) | collective-permute-done | bytes 524320 | tf_op jit(solution)/shard_map/while/body/eval_jaxpr/ppermute | solution.py:13
  985.8 14.2 %collective-permute-done.1 = bf16[64,4096]{1,0:T(8,128)(2,1)S(1)} collective-permute-done((bf16[64,4096]{1,0:T(8,128)(2,1)}, bf16[64,4096]{1,0:T(8,128)(2,1)S(1)}, u32[]{:S(2)}, u32[]{:S(2)}) %collective-permute-start.1) | collective-permute-done | bytes 524320 | tf_op jit(solution)/shard_map/while/body/eval_jaxpr/ppermute | solution.py:13
  1020.6 14.2 %collective-permute-done.1 = bf16[64,4096]{1,0:T(8,128)(2,1)S(1)} collective-permute-done((bf16[64,4096]{1,0:T(8,128)(2,1)}, bf16[64,4096]{1,0:T(8,128)(2,1)S(1)}, u32[]{:S(2)}, u32[]{:S(2)}) %collective-permute-start.1) | collective-permute-done | bytes 524320 | tf_op jit(solution)/shard_map/while/body/eval_jaxpr/ppermute | solution.py:13
  1055.4 14.1 %collective-permute-done.1 = bf16[64,4096]{1,0:T(8,128)(2,1)S(1)} collective-permute-done((bf16[64,4096]{1,0:T(8,128)(2,1)}, bf16[64,4096]{1,0:T(8,128)(2,1)S(1)}, u32[]{:S(2)}, u32[]{:S(2)}) %collective-permute-start.1) | collective-permute-done | bytes 524320 | tf_op jit(solution)/shard_map/while/body/eval_jaxpr/ppermute | solution.py:13
  1090.1 14.2 %collective-permute-done.1 = bf16[64,4096]{1,0:T(8,128)(2,1)S(1)} collective-permute-done((bf16[64,4096]{1,0:T(8,128)(2,1)}, bf16[64,4096]{1,0:T(8,128)(2,1)S(1)}, u32[]{:S(2)}, u32[]{:S(2)}) %collective-permute-start.1) | collective-permute-done | bytes 524320 | tf_op jit(solution)/shard_map/while/body/eval_jaxpr/ppermute | solution.py:13
  1124.9 14.2 %collective-permute-done.1 = bf16[64,4096]{1,0:T(8,128)(2,1)S(1)} collective-permute-done((bf16[64,4096]{1,0:T(8,128)(2,1)}, bf16[64,4096]{1,0:T(8,128)(2,1)S(1)}, u32[]{:S(2)}, u32[]{:S(2)}) %collective-permute-start.1) | collective-permute-done | bytes 524320 | tf_op jit(solution)/shard_map/while/body/eval_jaxpr/ppermute | solution.py:13
  1159.7 14.1 %collective-permute-done.1 = bf16[64,4096]{1,0:T(8,128)(2,1)S(1)} collective-permute-done((bf16[64,4096]{1,0:T(8,128)(2,1)}, bf16[64,4096]{1,0:T(8,128)(2,1)S(1)}, u32[]{:S(2)}, u32[]{:S(2)}) %collective-permute-start.1) | collective-permute-done | bytes 524320 | tf_op jit(solution)/shard_map/while/body/eval_jaxpr/ppermute | solution.py:13
  1194.5 14.2 %collective-permute-done.1 = bf16[64,4096]{1,0:T(8,128)(2,1)S(1)} collective-permute-done((bf16[64,4096]{1,0:T(8,128)(2,1)}, bf16[64,4096]{1,0:T(8,128)(2,1)S(1)}, u32[]{:S(2)}, u32[]{:S(2)}) %collective-permute-start.1) | collective-permute-done | bytes 524320 | tf_op jit(solution)/shard_map/while/body/eval_jaxpr/ppermute | solution.py:13
  1229.2 14.2 %collective-permute-done.1 = bf16[64,4096]{1,0:T(8,128)(2,1)S(1)} collective-permute-done((bf16[64,4096]{1,0:T(8,128)(2,1)}, bf16[64,4096]{1,0:T(8,128)(2,1)S(1)}, u32[]{:S(2)}, u32[]{:S(2)}) %collective-permute-start.1) | collective-permute-done | bytes 524320 | tf_op jit(solution)/shard_map/while/body/eval_jaxpr/ppermute | solution.py:13
  1264.0 14.2 %collective-permute-done.1 = bf16[64,4096]{1,0:T(8,128)(2,1)S(1)} collective-permute-done((bf16[64,4096]{1,0:T(8,128)(2,1)}, bf16[64,4096]{1,0:T(8,128)(2,1)S(1)}, u32[]{:S(2)}, u32[]{:S(2)}) %collective-permute-start.1) | collective-permute-done | bytes 524320 | tf_op jit(solution)/shard_map/while/body/eval_jaxpr/ppermute | solution.py:13
  1298.8 14.2 %collective-permute-done.1 = bf16[64,4096]{1,0:T(8,128)(2,1)S(1)} collective-permute-done((bf16[64,4096]{1,0:T(8,128)(2,1)}, bf16[64,4096]{1,0:T(8,128)(2,1)S(1)}, u32[]{:S(2)}, u32[]{:S(2)}) %collective-permute-start.1) | collective-permute-done | bytes 524320 | tf_op jit(solution)/shard_map/while/body/eval_jaxpr/ppermute | solution.py:13
  (577 shorter events, 925.9 us)
Async XLA Ops:
  713.6 23.1 %reduce-scatter.5.cloned.1.call-start = ((), (), s32[]{:S(2)}) async-start(), calls=%async_computation.3 | async-start | bytes 98304 | tf_op jit(solution)/shard_map/while/body/eval_jaxpr/reduce_scatter | solution.py:78
  741.0 15.6 %collective-permute-start.1 = (bf16[64,4096]{1,0:T(8,128)(2,1)}, bf16[64,4096]{1,0:T(8,128)(2,1)S(1)}, u32[]{:S(2)}, u32[]{:S(2)}) collective-permute-start(bf16[64,4096]{1,0:T(8,128)(2,1)} %fusion.71), channel_id=1, source_target_pairs={{2,0},{4,2},{6,4},{8,6},{10,8},{12,10},{14,12},{16,14},{18,16},{20... | collective-permute-start | bytes 1572872 | tf_op jit(solution)/shard_map/while/body/eval_jaxpr/ppermute | solution.py:13
  775.8 15.5 %collective-permute-start.1 = (bf16[64,4096]{1,0:T(8,128)(2,1)}, bf16[64,4096]{1,0:T(8,128)(2,1)S(1)}, u32[]{:S(2)}, u32[]{:S(2)}) collective-permute-start(bf16[64,4096]{1,0:T(8,128)(2,1)} %fusion.71), channel_id=1, source_target_pairs={{2,0},{4,2},{6,4},{8,6},{10,8},{12,10},{14,12},{16,14},{18,16},{20... | collective-permute-start | bytes 1572872 | tf_op jit(solution)/shard_map/while/body/eval_jaxpr/ppermute | solution.py:13
  810.5 15.5 %collective-permute-start.1 = (bf16[64,4096]{1,0:T(8,128)(2,1)}, bf16[64,4096]{1,0:T(8,128)(2,1)S(1)}, u32[]{:S(2)}, u32[]{:S(2)}) collective-permute-start(bf16[64,4096]{1,0:T(8,128)(2,1)} %fusion.71), channel_id=1, source_target_pairs={{2,0},{4,2},{6,4},{8,6},{10,8},{12,10},{14,12},{16,14},{18,16},{20... | collective-permute-start | bytes 1572872 | tf_op jit(solution)/shard_map/while/body/eval_jaxpr/ppermute | solution.py:13
  845.3 15.5 %collective-permute-start.1 = (bf16[64,4096]{1,0:T(8,128)(2,1)}, bf16[64,4096]{1,0:T(8,128)(2,1)S(1)}, u32[]{:S(2)}, u32[]{:S(2)}) collective-permute-start(bf16[64,4096]{1,0:T(8,128)(2,1)} %fusion.71), channel_id=1, source_target_pairs={{2,0},{4,2},{6,4},{8,6},{10,8},{12,10},{14,12},{16,14},{18,16},{20... | collective-permute-start | bytes 1572872 | tf_op jit(solution)/shard_map/while/body/eval_jaxpr/ppermute | solution.py:13
  860.9 15.1 %reduce-scatter.5.cloned.1.call-start = ((), (), s32[]{:S(2)}) async-start(), calls=%async_computation.3 | async-start | bytes 98304 | tf_op jit(solution)/shard_map/while/body/eval_jaxpr/reduce_scatter | solution.py:78
  880.1 15.5 %collective-permute-start.1 = (bf16[64,4096]{1,0:T(8,128)(2,1)}, bf16[64,4096]{1,0:T(8,128)(2,1)S(1)}, u32[]{:S(2)}, u32[]{:S(2)}) collective-permute-start(bf16[64,4096]{1,0:T(8,128)(2,1)} %fusion.71), channel_id=1, source_target_pairs={{2,0},{4,2},{6,4},{8,6},{10,8},{12,10},{14,12},{16,14},{18,16},{20... | collective-permute-start | bytes 1572872 | tf_op jit(solution)/shard_map/while/body/eval_jaxpr/ppermute | solution.py:13
  914.9 15.5 %collective-permute-start.1 = (bf16[64,4096]{1,0:T(8,128)(2,1)}, bf16[64,4096]{1,0:T(8,128)(2,1)S(1)}, u32[]{:S(2)}, u32[]{:S(2)}) collective-permute-start(bf16[64,4096]{1,0:T(8,128)(2,1)} %fusion.71), channel_id=1, source_target_pairs={{2,0},{4,2},{6,4},{8,6},{10,8},{12,10},{14,12},{16,14},{18,16},{20... | collective-permute-start | bytes 1572872 | tf_op jit(solution)/shard_map/while/body/eval_jaxpr/ppermute | solution.py:13
  949.6 15.5 %collective-permute-start.1 = (bf16[64,4096]{1,0:T(8,128)(2,1)}, bf16[64,4096]{1,0:T(8,128)(2,1)S(1)}, u32[]{:S(2)}, u32[]{:S(2)}) collective-permute-start(bf16[64,4096]{1,0:T(8,128)(2,1)} %fusion.71), channel_id=1, source_target_pairs={{2,0},{4,2},{6,4},{8,6},{10,8},{12,10},{14,12},{16,14},{18,16},{20... | collective-permute-start | bytes 1572872 | tf_op jit(solution)/shard_map/while/body/eval_jaxpr/ppermute | solution.py:13
  984.4 15.5 %collective-permute-start.1 = (bf16[64,4096]{1,0:T(8,128)(2,1)}, bf16[64,4096]{1,0:T(8,128)(2,1)S(1)}, u32[]{:S(2)}, u32[]{:S(2)}) collective-permute-start(bf16[64,4096]{1,0:T(8,128)(2,1)} %fusion.71), channel_id=1, source_target_pairs={{2,0},{4,2},{6,4},{8,6},{10,8},{12,10},{14,12},{16,14},{18,16},{20... | collective-permute-start | bytes 1572872 | tf_op jit(solution)/shard_map/while/body/eval_jaxpr/ppermute | solution.py:13
  999.9 15.1 %reduce-scatter.5.cloned.1.call-start = ((), (), s32[]{:S(2)}) async-start(), calls=%async_computation.3 | async-start | bytes 98304 | tf_op jit(solution)/shard_map/while/body/eval_jaxpr/reduce_scatter | solution.py:78
  1019.2 15.5 %collective-permute-start.1 = (bf16[64,4096]{1,0:T(8,128)(2,1)}, bf16[64,4096]{1,0:T(8,128)(2,1)S(1)}, u32[]{:S(2)}, u32[]{:S(2)}) collective-permute-start(bf16[64,4096]{1,0:T(8,128)(2,1)} %fusion.71), channel_id=1, source_target_pairs={{2,0},{4,2},{6,4},{8,6},{10,8},{12,10},{14,12},{16,14},{18,16},{20... | collective-permute-start | bytes 1572872 | tf_op jit(solution)/shard_map/while/body/eval_jaxpr/ppermute | solution.py:13
  1034.7 15.1 %reduce-scatter.5.cloned.1.call-start = ((), (), s32[]{:S(2)}) async-start(), calls=%async_computation.3 | async-start | bytes 98304 | tf_op jit(solution)/shard_map/while/body/eval_jaxpr/reduce_scatter | solution.py:78
  1054.0 15.5 %collective-permute-start.1 = (bf16[64,4096]{1,0:T(8,128)(2,1)}, bf16[64,4096]{1,0:T(8,128)(2,1)S(1)}, u32[]{:S(2)}, u32[]{:S(2)}) collective-permute-start(bf16[64,4096]{1,0:T(8,128)(2,1)} %fusion.71), channel_id=1, source_target_pairs={{2,0},{4,2},{6,4},{8,6},{10,8},{12,10},{14,12},{16,14},{18,16},{20... | collective-permute-start | bytes 1572872 | tf_op jit(solution)/shard_map/while/body/eval_jaxpr/ppermute | solution.py:13
  1069.5 15.1 %reduce-scatter.5.cloned.1.call-start = ((), (), s32[]{:S(2)}) async-start(), calls=%async_computation.3 | async-start | bytes 98304 | tf_op jit(solution)/shard_map/while/body/eval_jaxpr/reduce_scatter | solution.py:78
  1088.8 15.5 %collective-permute-start.1 = (bf16[64,4096]{1,0:T(8,128)(2,1)}, bf16[64,4096]{1,0:T(8,128)(2,1)S(1)}, u32[]{:S(2)}, u32[]{:S(2)}) collective-permute-start(bf16[64,4096]{1,0:T(8,128)(2,1)} %fusion.71), channel_id=1, source_target_pairs={{2,0},{4,2},{6,4},{8,6},{10,8},{12,10},{14,12},{16,14},{18,16},{20... | collective-permute-start | bytes 1572872 | tf_op jit(solution)/shard_map/while/body/eval_jaxpr/ppermute | solution.py:13
  1123.6 15.5 %collective-permute-start.1 = (bf16[64,4096]{1,0:T(8,128)(2,1)}, bf16[64,4096]{1,0:T(8,128)(2,1)S(1)}, u32[]{:S(2)}, u32[]{:S(2)}) collective-permute-start(bf16[64,4096]{1,0:T(8,128)(2,1)} %fusion.71), channel_id=1, source_target_pairs={{2,0},{4,2},{6,4},{8,6},{10,8},{12,10},{14,12},{16,14},{18,16},{20... | collective-permute-start | bytes 1572872 | tf_op jit(solution)/shard_map/while/body/eval_jaxpr/ppermute | solution.py:13
  1139.1 15.1 %reduce-scatter.5.cloned.1.call-start = ((), (), s32[]{:S(2)}) async-start(), calls=%async_computation.3 | async-start | bytes 98304 | tf_op jit(solution)/shard_map/while/body/eval_jaxpr/reduce_scatter | solution.py:78
  1158.4 15.5 %collective-permute-start.1 = (bf16[64,4096]{1,0:T(8,128)(2,1)}, bf16[64,4096]{1,0:T(8,128)(2,1)S(1)}, u32[]{:S(2)}, u32[]{:S(2)}) collective-permute-start(bf16[64,4096]{1,0:T(8,128)(2,1)} %fusion.71), channel_id=1, source_target_pairs={{2,0},{4,2},{6,4},{8,6},{10,8},{12,10},{14,12},{16,14},{18,16},{20... | collective-permute-start | bytes 1572872 | tf_op jit(solution)/shard_map/while/body/eval_jaxpr/ppermute | solution.py:13
  1173.8 15.1 %reduce-scatter.5.cloned.1.call-start = ((), (), s32[]{:S(2)}) async-start(), calls=%async_computation.3 | async-start | bytes 98304 | tf_op jit(solution)/shard_map/while/body/eval_jaxpr/reduce_scatter | solution.py:78
  1193.1 15.5 %collective-permute-start.1 = (bf16[64,4096]{1,0:T(8,128)(2,1)}, bf16[64,4096]{1,0:T(8,128)(2,1)S(1)}, u32[]{:S(2)}, u32[]{:S(2)}) collective-permute-start(bf16[64,4096]{1,0:T(8,128)(2,1)} %fusion.71), channel_id=1, source_target_pairs={{2,0},{4,2},{6,4},{8,6},{10,8},{12,10},{14,12},{16,14},{18,16},{20... | collective-permute-start | bytes 1572872 | tf_op jit(solution)/shard_map/while/body/eval_jaxpr/ppermute | solution.py:13
  1227.9 15.5 %collective-permute-start.1 = (bf16[64,4096]{1,0:T(8,128)(2,1)}, bf16[64,4096]{1,0:T(8,128)(2,1)S(1)}, u32[]{:S(2)}, u32[]{:S(2)}) collective-permute-start(bf16[64,4096]{1,0:T(8,128)(2,1)} %fusion.71), channel_id=1, source_target_pairs={{2,0},{4,2},{6,4},{8,6},{10,8},{12,10},{14,12},{16,14},{18,16},{20... | collective-permute-start | bytes 1572872 | tf_op jit(solution)/shard_map/while/body/eval_jaxpr/ppermute | solution.py:13
  1262.7 15.5 %collective-permute-start.1 = (bf16[64,4096]{1,0:T(8,128)(2,1)}, bf16[64,4096]{1,0:T(8,128)(2,1)S(1)}, u32[]{:S(2)}, u32[]{:S(2)}) collective-permute-start(bf16[64,4096]{1,0:T(8,128)(2,1)} %fusion.71), channel_id=1, source_target_pairs={{2,0},{4,2},{6,4},{8,6},{10,8},{12,10},{14,12},{16,14},{18,16},{20... | collective-permute-start | bytes 1572872 | tf_op jit(solution)/shard_map/while/body/eval_jaxpr/ppermute | solution.py:13
  1297.5 15.5 %collective-permute-start.1 = (bf16[64,4096]{1,0:T(8,128)(2,1)}, bf16[64,4096]{1,0:T(8,128)(2,1)S(1)}, u32[]{:S(2)}, u32[]{:S(2)}) collective-permute-start(bf16[64,4096]{1,0:T(8,128)(2,1)} %fusion.71), channel_id=1, source_target_pairs={{2,0},{4,2},{6,4},{8,6},{10,8},{12,10},{14,12},{16,14},{18,16},{20... | collective-permute-start | bytes 1572872 | tf_op jit(solution)/shard_map/while/body/eval_jaxpr/ppermute | solution.py:13
  (82 other events, 2713.2 us)
Sparse Core Ops, SparseCore 0:
  122.5 10.0 reduce-scatter.2
  157.2 10.0 reduce-scatter.2
  191.7 10.0 reduce-scatter.2
  226.4 10.0 reduce-scatter.2
  295.6 10.0 reduce-scatter.2
  364.8 10.0 reduce-scatter.2
  399.4 10.0 reduce-scatter.2
  718.5 18.2 reduce-scatter.4
  761.4 10.1 reduce-scatter.4
  796.1 10.1 reduce-scatter.4
  830.9 10.1 reduce-scatter.4
  865.7 10.1 reduce-scatter.4
  900.5 10.1 reduce-scatter.4
  935.3 10.1 reduce-scatter.4
  970.1 10.1 reduce-scatter.4
  1004.8 10.2 reduce-scatter.4
  1039.6 10.2 reduce-scatter.4
  1074.3 10.2 reduce-scatter.4
  1109.2 10.1 reduce-scatter.4
  1143.9 10.2 reduce-scatter.4
  1178.7 10.2 reduce-scatter.4
  1213.5 10.1 reduce-scatter.4
  1248.3 10.1 reduce-scatter.4
  1283.1 10.1 reduce-scatter.4
  (10 shorter events, 99.5 us)
where the time goes:
time: 1340 us; the launch traced here: 1330 us
  waiting for transfers between devices  767 us (57%)
  blocking collectives  166 us (12%)
  matrix products  131 us (10%)
  other arithmetic  102 us (8%)
  starting transfers between devices  81.2 us (6%)
  local copies, waits for them, and re-layouts  64.4 us (5%)
  between operations  14.7 us (1%)
    ppermute x34, waiting for transfers between devices, shifted(): lax.ppermute(value, axis, [(source, source + steps) for source in range(l...  428 us
    reduce_scatter x17, waiting for transfers between devices, backward_act(): lax.psum_scatter(partial_sum, 'tp', scatter_dimension=1, tiled=True)  184 us
    reduce_scatter x17, waiting for transfers between devices, forward_act(): lax.psum_scatter(partial_sum, 'tp', scatter_dimension=1, tiled=True)  154 us
    ppermute x34, starting transfers between devices, shifted(): lax.ppermute(value, axis, [(source, source + steps) for source in range(l...  81.1 us
    dynamic_update_slice x85, other arithmetic, place_row(): lax.dynamic_update_index_in_dim(stack, jnp.where(active, new_value, previ...  71 us
    unnamed x1, blocking collectives  61.8 us
    dynamic_slice x102, local copies, waits for them, and re-layouts, place_row(): previous = lax.dynamic_index_in_dim(stack, index_value, 0, keepdims=False)  58.1 us
    dot_general x17, matrix products, forward_tick(): jnp.dot(activated, up_local, preferred_element_type=jnp.float32)  50 us
  transfers between devices with their start and end apart: 68, of which 68 were waited for; matrix products, arithmetic and copies ran while one was open for 1% of the time, Pallas kernels for 0%

commit v1 on v0

v1 whole, which is shorter than its diff:
```python
import functools

import jax
import jax.numpy as jnp
from jax import lax
from jax.experimental import pallas as pl
from jax.experimental.pallas import tpu as pltpu
from jax.sharding import PartitionSpec as P

MESH = pl.DeviceIdType.MESH
CHUNK = 16
PIECES = 4
NT = (((1,), (1,)), ((), ()))


def derivative(pre_act):
    s = jax.nn.sigmoid(pre_act)
    return s * (1.0 + pre_act * (1.0 - s))


def kernel(
    n_pipe,
    n_tp,
    batch,
    hidden,
    rewards,
    counts,
    episode,
    down,
    up,
    head,
    h_out,
    act_out,
    pg_out,
    g_out,
    msg_out,
    h_buf,
    o_buf,
    g_buf,
    q_buf,
    act_buf,
    pg_buf,
    pre_buf,
    fx,
    bx,
    vx,
    w_buf,
    aux,
    msg,
    msg_in,
    f_send,
    f_recv,
    b_send,
    b_recv,
    fx_send,
    fx_recv,
    bx_send,
    bx_recv,
    vx_send,
    vx_recv,
    msg_send,
    msg_recv,
    local_sem,
):
    p = lax.axis_index("pipe")
    me = lax.axis_index("tp")
    last = n_pipe - 1
    is_last = p == last
    rows, width = h_buf.shape
    inner = down.shape[1]
    chunks = rows // CHUNK
    piece = width // PIECES
    peers = [lax.rem(me + i, n_tp) for i in range(1, n_tp)]
    block = msg.shape[2]

    def to_pipe(q):
        return {"pipe": q, "tp": me}

    def to_peer(t):
        return {"pipe": p, "tp": t}

    barrier = pltpu.get_barrier_semaphore()
    for t in peers:
        pl.semaphore_signal(barrier, inc=1, device_id=to_peer(t), device_id_type=MESH)

    @pl.when(p > 0)
    def _():
        pl.semaphore_signal(barrier, inc=1, device_id=to_pipe(p - 1), device_id_type=MESH)

    @pl.when(p < last)
    def _():
        pl.semaphore_signal(barrier, inc=1, device_id=to_pipe(p + 1), device_id_type=MESH)
        pl.semaphore_signal(barrier, inc=1, device_id=to_pipe(last), device_id_type=MESH)

    @pl.when(is_last)
    def _():
        def greet(q, carry):
            pl.semaphore_signal(barrier, inc=1, device_id=to_pipe(q), device_id_type=MESH)
            return carry

        lax.fori_loop(0, last, greet, 0)

    @pl.when(p == 0)
    def _():
        pl.semaphore_wait(barrier, n_tp + 1)

    @pl.when((p > 0) & (p < last))
    def _():
        pl.semaphore_wait(barrier, n_tp + 2)

    @pl.when(is_last)
    def _():
        pl.semaphore_wait(barrier, n_tp + last)

    @pl.when(p == 0)
    def _():
        copy = pltpu.make_async_copy(hidden, h_buf, local_sem.at[0])
        copy.start()
        copy.wait()

    @pl.when(is_last)
    def _():
        shape = (rows, rows)
        i = lax.broadcasted_iota(jnp.int32, shape, 0)
        j = lax.broadcasted_iota(jnp.int32, shape, 1)
        cap = rows // batch

        def per_slot(idx):
            live = jnp.zeros(shape, jnp.float32)
            next_live = jnp.zeros(shape, jnp.float32)
            owner = jnp.zeros(shape, jnp.int32)
            for m in range(batch):
                inside = (idx >= m * cap) & (idx < (m + 1) * cap)
                slot = idx - m * cap
                live = jnp.where(inside & (slot < counts[m]), 1.0, live)
                next_live = jnp.where(inside & (slot + 1 < counts[m]), 1.0, next_live)
                owner = jnp.where(inside, m, owner)
            return live, next_live, owner

        live_i, _, owner_i = per_slot(i)
        live_j, next_live_j, owner_j = per_slot(j)
        ep_j = jnp.broadcast_to(episode[...].astype(jnp.float32), shape)
        ep_i = jnp.broadcast_to(
            jnp.sum(jnp.where(i == j, ep_j, 0.0), axis=1, keepdims=True), shape
        )
        keep = (j >= i) & (ep_i == ep_j) & (owner_i == owner_j)
        w_buf[...] = jnp.where(keep, live_i * live_j, 0.0)
        ep_next = jnp.broadcast_to(
            jnp.sum(jnp.where(i == j + 1, ep_i, 0.0), axis=0, keepdims=True), shape
        )
        follow = jnp.where(ep_next == ep_j, next_live_j, 0.0)
        aux[0:8, :] = live_j[0:8]
        aux[8:16, :] = follow[0:8]

    def exchange_start(buf, send, recv, rs, c):
        for t in peers:
            pltpu.make_async_remote_copy(
                src_ref=buf.at[me, rs],
                dst_ref=buf.at[me, rs],
                send_sem=send.at[c, t],
                recv_sem=recv.at[c, me],
                device_id=to_peer(t),
                device_id_type=MESH,
            ).start()

    def exchange_wait(buf, send, recv, rs, c):
        for t in peers:
            pltpu.make_async_remote_copy(
                src_ref=buf.at[t, rs],
                dst_ref=buf.at[t, rs],
                send_sem=send.at[c, t],
                recv_sem=recv.at[c, t],
                device_id=to_peer(t),
                device_id_type=MESH,
            ).wait_recv()

    def exchange_done(buf, send, recv, rs, c):
        for t in peers:
            pltpu.make_async_remote_copy(
                src_ref=buf.at[me, rs],
                dst_ref=buf.at[me, rs],
                send_sem=send.at[c, t],
                recv_sem=recv.at[c, me],
                device_id=to_peer(t),
                device_id_type=MESH,
            ).wait_send()

    def total_of(buf, rs):
        total = buf[0, rs]
        for t in range(1, n_tp):
            total += buf[t, rs]
        return total

    def rows_of(c):
        return pl.ds(pl.multiple_of(c * CHUNK, CHUNK), CHUNK)

    def cols_of(s):
        return pl.ds(s * piece, piece)

    def forward_copy(c, s, target):
        return pltpu.make_async_remote_copy(
            src_ref=o_buf.at[rows_of(c), cols_of(s)],
            dst_ref=h_buf.at[rows_of(c), cols_of(s)],
            send_sem=f_send.at[c, s],
            recv_sem=f_recv.at[c, s],
            device_id=to_pipe(target),
            device_id_type=MESH,
        )

    def backward_copy(c, s, target):
        return pltpu.make_async_remote_copy(
            src_ref=q_buf.at[rows_of(c), cols_of(s)],
            dst_ref=g_buf.at[rows_of(c), cols_of(s)],
            send_sem=b_send.at[c, s],
            recv_sem=b_recv.at[c, s],
            device_id=to_pipe(target),
            device_id_type=MESH,
        )

    def forward(c, carry):
        rs = rows_of(c)
        total = jnp.zeros((CHUNK, inner), jnp.float32)
        for s in range(PIECES):

            @pl.when(p > 0)
            def _():
                forward_copy(c, s, p - 1).wait_recv()

            total += jnp.dot(
                h_buf[rs, cols_of(s)], down[cols_of(s), :], preferred_element_type=jnp.float32
            )
        fx[me, rs] = total
        exchange_start(fx, fx_send, fx_recv, rs, c)
        exchange_wait(fx, fx_send, fx_recv, rs, c)
        pre = total_of(fx, rs)
        act = jax.nn.silu(pre).astype(jnp.bfloat16)
        for s in range(PIECES):
            out = h_buf[rs, cols_of(s)].astype(jnp.float32) + jnp.dot(
                act, up[:, cols_of(s)], preferred_element_type=jnp.float32
            )
            o_buf[rs, cols_of(s)] = out.astype(jnp.bfloat16)

            @pl.when(p < last)
            def _():
                forward_copy(c, s, p + 1).start()

        pre_buf[rs] = pre
        act_buf[rs] = act

        @pl.when(is_last)
        def _():
            value = jnp.zeros((CHUNK, 1), jnp.float32)
            for s in range(PIECES):
                value += jnp.sum(
                    o_buf[rs, cols_of(s)].astype(jnp.float32)
                    * head[:, cols_of(s)].astype(jnp.float32),
                    axis=1,
                    keepdims=True,
                )
            vx[me, rs] = jnp.broadcast_to(value, (CHUNK, vx.shape[2]))

        return carry

    lax.fori_loop(0, chunks, forward, 0)

    every = pl.ds(0, rows)
    copies = [
        pltpu.make_async_copy(h_buf, h_out, local_sem.at[0]),
        pltpu.make_async_copy(act_buf, act_out, local_sem.at[1]),
    ]
    for copy in copies:
        copy.start()

    @pl.when(is_last)
    def _():
        exchange_start(vx, vx_send, vx_recv, every, 0)
        exchange_wait(vx, vx_send, vx_recv, every, 0)
        shape = (rows, rows)
        i = lax.broadcasted_iota(jnp.int32, shape, 0)
        j = lax.broadcasted_iota(jnp.int32, shape, 1)
        value = jnp.broadcast_to(total_of(vx, every)[:, 0:1], shape)
        value_row = jnp.sum(jnp.where(i == j, value, 0.0), axis=0, keepdims=True)
        next_row = jnp.sum(jnp.where(i == j + 1, value, 0.0), axis=0, keepdims=True)
        delta = (rewards[...] + aux[8:9, :] * next_row - value_row) * aux[0:1, :]
        adv = jnp.sum(w_buf[...] * delta, axis=1, keepdims=True)
        adv_all = jnp.broadcast_to(adv, shape)
        w_buf[...] = adv_all
        aux[0:8, :] = jnp.broadcast_to(
            jnp.sum(jnp.where(i == j, adv_all, 0.0), axis=0, keepdims=True), (8, rows)
        )
        for s in range(PIECES):
            g_buf[:, cols_of(s)] = (-adv * head[:, cols_of(s)].astype(jnp.float32)).astype(
                jnp.bfloat16
            )

    def backward(c, carry):
        rs = rows_of(c)
        total = jnp.zeros((CHUNK, inner), jnp.float32)
        for s in range(PIECES):

            @pl.when(p < last)
            def _():
                backward_copy(c, s, p + 1).wait_recv()

            total += lax.dot_general(
                g_buf[rs, cols_of(s)], up[:, cols_of(s)], NT, preferred_element_type=jnp.float32
            )
        bx[me, rs] = total
        exchange_start(bx, bx_send, bx_recv, rs, c)
        slope = derivative(pre_buf[rs])
        exchange_wait(bx, bx_send, bx_recv, rs, c)
        pg = (total_of(bx, rs) * slope).astype(jnp.bfloat16)

        @pl.when(p > 0)
        def _():
            for s in range(PIECES):
                out = g_buf[rs, cols_of(s)].astype(jnp.float32) + lax.dot_general(
                    pg, down[cols_of(s), :], NT, preferred_element_type=jnp.float32
                )
                q_buf[rs, cols_of(s)] = out.astype(jnp.bfloat16)
                backward_copy(c, s, p - 1).start()

        pg_buf[rs] = pg
        return carry

    lax.fori_loop(0, chunks, backward, 0)

    ends = [
        pltpu.make_async_copy(g_buf, g_out, local_sem.at[2]),
        pltpu.make_async_copy(pg_buf, pg_out, local_sem.at[3]),
    ]
    for copy in ends:
        copy.start()

    slice_width = width // n_pipe

    def message_copy(q):
        return pltpu.make_async_remote_copy(
            src_ref=msg.at[q],
            dst_ref=msg_in,
            send_sem=msg_send.at[q],
            recv_sem=msg_recv.at[0],
            device_id=to_pipe(q),
            device_id_type=MESH,
        )

    @pl.when(is_last)
    def _():
        adv_row = aux[0:1, :]
        adv = w_buf[:, 0:1]
        for b in range(width // block):
            cs = pl.ds(b * block, block)
            head_grad = jnp.sum(o_buf[:, cs].astype(jnp.float32) * -adv, axis=0, keepdims=True)
            for q in range(n_pipe):
                if q * slice_width // block == b:
                    msg[q, 0:1, :] = head_grad
                    msg[q, 1:2, 0:rows] = adv_row
        for q in range(last):
            message_copy(q).start()
        msg_out[...] = msg[last]

    @pl.when(p < last)
    def _():
        message_copy(last).wait_recv()
        msg_out[...] = msg_in[...]

    def finish(c, carry):
        rs = rows_of(c)
        for s in range(PIECES):

            @pl.when(p < last)
            def _():
                forward_copy(c, s, p + 1).wait_send()

            @pl.when(p > 0)
            def _():
                backward_copy(c, s, p - 1).wait_send()

        exchange_done(fx, fx_send, fx_recv, rs, c)
        exchange_done(bx, bx_send, bx_recv, rs, c)
        return carry

    lax.fori_loop(0, chunks, finish, 0)

    @pl.when(is_last)
    def _():
        exchange_done(vx, vx_send, vx_recv, every, 0)
        for q in range(last):
            message_copy(q).wait_send()

    for copy in copies + ends:
        copy.wait()


def local(hidden, rewards, counts, episode, down_weight, up_weight, head_weight):
    n_pipe = lax.axis_size("pipe")
    n_tp = lax.axis_size("tp")
    batch, cap, width = hidden.shape
    rows = batch * cap
    down, up = down_weight[0], up_weight[0]
    inner = down.shape[1]
    chunks = rows // CHUNK
    slice_width = width // n_pipe
    block = max(slice_width, 128)
    bf16, f32 = jnp.bfloat16, jnp.float32
    vmem = pl.BlockSpec(memory_space=pltpu.VMEM)
    smem = pl.BlockSpec(memory_space=pltpu.SMEM)
    anywhere = pl.BlockSpec(memory_space=pl.ANY)
    dma = pltpu.SemaphoreType.DMA
    h, act, pg, g, msg = pl.pallas_call(
        functools.partial(kernel, n_pipe, n_tp, batch),
        out_shape=(
            jax.ShapeDtypeStruct((rows, width), bf16),
            jax.ShapeDtypeStruct((rows, inner), bf16),
            jax.ShapeDtypeStruct((rows, inner), bf16),
            jax.ShapeDtypeStruct((rows, width), bf16),
            jax.ShapeDtypeStruct((8, block), f32),
        ),
        in_specs=[anywhere, vmem, smem, vmem, vmem, vmem, vmem],
        out_specs=(anywhere, anywhere, anywhere, anywhere, vmem),
        scratch_shapes=[
            pltpu.VMEM((rows, width), bf16),
            pltpu.VMEM((rows, width), bf16),
            pltpu.VMEM((rows, width), bf16),
            pltpu.VMEM((rows, width), bf16),
            pltpu.VMEM((rows, inner), bf16),
            pltpu.VMEM((rows, inner), bf16),
            pltpu.VMEM((rows, inner), f32),
            pltpu.VMEM((n_tp, rows, inner), f32),
            pltpu.VMEM((n_tp, rows, inner), f32),
            pltpu.VMEM((n_tp, rows, 128), f32),
            pltpu.VMEM((rows, rows), f32),
            pltpu.VMEM((16, rows), f32),
            pltpu.VMEM((n_pipe, 8, block), f32),
            pltpu.VMEM((8, block), f32),
            dma((chunks, PIECES)),
            dma((chunks, PIECES)),
            dma((chunks, PIECES)),
            dma((chunks, PIECES)),
            dma((chunks, n_tp)),
            dma((chunks, n_tp)),
            dma((chunks, n_tp)),
            dma((chunks, n_tp)),
            dma((1, n_tp)),
            dma((1, n_tp)),
            dma((n_pipe,)),
            dma((1,)),
            dma((4,)),
        ],
        compiler_params=pltpu.CompilerParams(
            collective_id=0, has_side_effects=True, vmem_limit_bytes=40 * 1024 * 1024
        ),
        name="adapters",
    )(
        hidden.reshape(rows, width),
        rewards.reshape(1, rows),
        counts,
        episode.reshape(1, rows),
        down,
        up,
        head_weight.reshape(1, width),
    )
    grad_down = jnp.einsum("nd,nk->dk", h, pg, preferred_element_type=f32)
    grad_up = jnp.einsum("nk,nd->kd", act, g, preferred_element_type=f32)
    offset = lax.rem(lax.axis_index("pipe") * slice_width, block)
    grad_head = lax.dynamic_slice(msg, (0, offset), (1, slice_width))
    advantages = msg[1, :rows].reshape(batch, cap)
    return (grad_down[None], grad_up[None], grad_head[None].reshape(1, slice_width), advantages)


def solution(mesh):
    return jax.shard_map(
        local,
        mesh=mesh,
        in_specs=(
            P(None, None, "tp"),
            P(),
            P(),
            P(),
            P("pipe", "tp", None),
            P("pipe", None, "tp"),
            P("tp"),
        ),
        out_specs=(P("pipe", "tp", None), P("pipe", None, "tp"), P("tp", "pipe"), P()),
        check_vma=False,
    )
```

time: 1340 us -> 276 us (0.21)
  waiting for transfers between devices: 767 us -> 0 us
  Pallas kernels: 0 us -> 261 us
  blocking collectives: 166 us -> 0 us
  matrix products: 131 us -> 5.49 us
  other arithmetic: 102 us -> 0 us
  starting transfers between devices: 81.2 us -> 0 us
  local copies, waits for them, and re-layouts: 64.4 us -> 8.5 us
  between operations: 14.7 us -> 0.66 us
    ppermute x34 -> x0, waiting for transfers between devices: 428 us -> none  [shifted(): lax.ppermute(value, axis, [(source, source + steps) for source in range(l...]
    reduce_scatter x34 -> x0, waiting for transfers between devices: 338 us -> none  [the longest x17 184 us: backward_act(): lax.psum_scatter(partial_sum, 'tp', scatter_dimension=1, tiled=True)]
    pallas_call x0 -> x1, Pallas kernels: none -> 261 us  [local(): pl.pallas_call(functools.partial(kernel, n_pipe, n_tp, batch), out_shape=...]
    dot_general x73 -> x2, matrix products: 131 us -> 5.49 us  [the longest x1 2.75 us: local(): grad_down = jnp.einsum('nd,nk->dk', h, pg, preferred_element_type=f32)]
    ppermute x34 -> x0, starting transfers between devices: 81.1 us -> none  [shifted(): lax.ppermute(value, axis, [(source, source + steps) for source in range(l...]
    dynamic_update_slice x85 -> x0, other arithmetic: 71 us -> none  [place_row(): lax.dynamic_update_index_in_dim(stack, jnp.where(active, new_value, previ...]
    all_gather x34 -> x0, blocking collectives: 62.2 us -> none  [the longest x17 31.1 us: backward_act(): lax.all_gather((share_sum * derivative(pre_act)).astype(jnp.bfloat16), 't...]
    unnamed x1 -> x0, blocking collectives: 61.8 us -> none
  transfers between devices with their start and end apart: 68 -> 0, of which waited for: 68 -> 0; matrix products, arithmetic and copies ran while one was open for 1% -> 0% of each run, Pallas kernels for 0% -> 0%
where the time goes in v1:
time: 276 us
  Pallas kernels  261 us (95%)
  local copies, waits for them, and re-layouts  8.5 us (3%)
  matrix products  5.49 us (2%)
    pallas_call x1, Pallas kernels, local(): pl.pallas_call(functools.partial(kernel, n_pipe, n_tp, batch), out_shape=...  261 us

profile of v1, /device:TPU:1, one launch (start us, length us, event | category | flops | bytes accessed | tf_op | source)
XLA Modules:
  0.0 275.8 jit_solution(9590750028758020348)
XLA Ops:
  0.6 0.8 reshape.21.rewards
  1.4 0.8 reshape.22.episode
  2.1 0.7 reshape.23.head
  2.9 0.0 copy-start
  2.9 1.6 copy-done
  4.5 0.0 copy-start.1
  4.5 1.6 copy-done.1
  6.0 0.0 copy-start.2
  6.0 1.2 copy-done.2
  7.3 0.0 copy-start.3
  7.3 0.7 copy-done.3
  7.9 261.2 %adapters.1 = (bf16[128,4096]{1,0:T(8,128)(2,1)S(1)}, bf16[128,256]{1,0:T(8,128)(2,1)S(1)}, bf16[128,256]{1,0:T(8,128)(2,1)S(1)}, bf16[128,4096]{1,0:T(8,128)(2,1)S(1)}, f32[8,256]{1,0:T(8,128)S(1)}) custom-call(bf16[128,4096]{1,0:T(8,128)(2,1)S(1)} %bitcast.13, f32[1,128]{1,0:T(1,128)S(1)} %reshape.21.rewards, s32[2]{0:T(128)S(1)} %copy-done.3, ...), custom_call_target="tpu_custom_call" | custom-call | tf_op jit(solution)/shard_map/adapters/pallas_call | solution.py:410
  269.1 0.6 dynamic_slice.4
  269.7 0.6 reshape_squeeze.3
  270.3 2.8 convolution_bitcast_fusion.1
  273.1 2.7 convolution_bitcast_fusion
  (1 shorter events, 0.0 us)
Async XLA Ops:
  2.9 1.6 copy-start
  4.5 1.6 copy-start.1
  6.0 1.2 copy-start.2
  7.3 0.7 copy-start.3

commit v2 on v1

v2 whole, which is shorter than its diff:
```python
import functools

import jax
import jax.numpy as jnp
from jax import lax
from jax.experimental import pallas as pl
from jax.experimental.pallas import tpu as pltpu
from jax.sharding import PartitionSpec as P

MESH = pl.DeviceIdType.MESH
CHUNK = 8
PIECES = 4


def derivative(pre_act):
    s = jax.nn.sigmoid(pre_act)
    return s * (1.0 + pre_act * (1.0 - s))


def kernel(
    n_pipe,
    n_tp,
    batch,
    hidden,
    rewards,
    counts,
    episode,
    down,
    up,
    head,
    h_out,
    act_out,
    pg_out,
    g_out,
    msg_out,
    hid,
    h_buf,
    o_buf,
    g_buf,
    q_buf,
    flat,
    narrow,
    act_buf,
    pg_buf,
    pre_buf,
    wd,
    wu,
    wd_t,
    wu_t,
    hd,
    o_sum,
    ghx,
    vx,
    w_buf,
    aux,
    msg,
    msg_in,
    f_send,
    f_recv,
    b_send,
    b_recv,
    gx_send,
    gx_recv,
    px_send,
    px_recv,
    x_send,
    x_recv,
    msg_send,
    msg_recv,
    local_sem,
):
    p = lax.axis_index("pipe")
    me = lax.axis_index("tp")
    last = n_pipe - 1
    is_last = p == last
    width = h_buf.shape[1]
    rows = vx.shape[0]
    inner = wd.shape[2]
    own = rows // n_tp
    chunks = own // CHUNK
    fold = CHUNK * n_tp
    piece = width // PIECES
    peers = [lax.rem(me + i, n_tp) for i in range(1, n_tp)]
    block = msg.shape[2]
    sent = hid.shape[1]
    bf16, f32 = jnp.bfloat16, jnp.float32

    def to_pipe(q):
        return {"pipe": q, "tp": me}

    def to_peer(t):
        return {"pipe": p, "tp": t}

    barrier = pltpu.get_barrier_semaphore()
    for t in peers:
        pl.semaphore_signal(barrier, inc=1, device_id=to_peer(t), device_id_type=MESH)

    @pl.when(p > 0)
    def _():
        pl.semaphore_signal(barrier, inc=1, device_id=to_pipe(p - 1), device_id_type=MESH)

    @pl.when(p < last)
    def _():
        pl.semaphore_signal(barrier, inc=1, device_id=to_pipe(p + 1), device_id_type=MESH)
        pl.semaphore_signal(barrier, inc=1, device_id=to_pipe(last), device_id_type=MESH)

    @pl.when(is_last)
    def _():
        def greet(q, carry):
            pl.semaphore_signal(barrier, inc=1, device_id=to_pipe(q), device_id_type=MESH)
            return carry

        lax.fori_loop(0, last, greet, 0)

    @pl.when(p == 0)
    def _():
        pl.semaphore_wait(barrier, n_tp + 1)

    @pl.when((p > 0) & (p < last))
    def _():
        pl.semaphore_wait(barrier, n_tp + 2)

    @pl.when(is_last)
    def _():
        pl.semaphore_wait(barrier, n_tp + last)

    def peer_copy(src, dst, kind, t, slot):
        return pltpu.make_async_remote_copy(
            src_ref=src,
            dst_ref=dst,
            send_sem=x_send.at[kind, t],
            recv_sem=x_recv.at[kind, slot],
            device_id=to_peer(t),
            device_id_type=MESH,
        )

    def head_copy(t, slot):
        rs = pl.ds(pl.multiple_of(slot * CHUNK, CHUNK), CHUNK)
        return peer_copy(hd.at[rs], hd.at[rs], 6, t, slot)

    def from_row(t):
        return pl.multiple_of(t * own, own) if sent == own else 0

    def hidden_copy(t, slot):
        return peer_copy(hidden.at[pl.ds(from_row(t), sent)], hid.at[slot], 0, t, slot)

    loads = [
        pltpu.make_async_copy(down, wd.at[me], local_sem.at[0]),
        pltpu.make_async_copy(up, wu.at[me], local_sem.at[1]),
    ]
    own_hidden = pltpu.make_async_copy(
        hidden.at[pl.ds(from_row(me), sent)], hid.at[me], local_sem.at[2]
    )

    @pl.when(p == 0)
    def _():
        own_hidden.start()
        for t in peers:
            hidden_copy(t, me).start()

    for t in peers:
        peer_copy(down, wd.at[me], 1, t, me).start()
    loads[0].start()
    for t in peers:
        peer_copy(up, wu.at[me], 2, t, me).start()
    loads[1].start()

    @pl.when(is_last)
    def _():
        hd[pl.ds(pl.multiple_of(me * CHUNK, CHUNK), CHUNK), :] = jnp.broadcast_to(
            head[...].astype(f32), (CHUNK, width)
        )
        for t in peers:
            head_copy(t, me).start()

    @pl.when(is_last)
    def _():
        shape = (rows, rows)
        i = lax.broadcasted_iota(jnp.int32, shape, 0)
        j = lax.broadcasted_iota(jnp.int32, shape, 1)
        cap = rows // batch

        def per_slot(idx):
            live = jnp.zeros(shape, jnp.float32)
            next_live = jnp.zeros(shape, jnp.float32)
            owner = jnp.zeros(shape, jnp.int32)
            for m in range(batch):
                inside = (idx >= m * cap) & (idx < (m + 1) * cap)
                slot = idx - m * cap
                live = jnp.where(inside & (slot < counts[m]), 1.0, live)
                next_live = jnp.where(inside & (slot + 1 < counts[m]), 1.0, next_live)
                owner = jnp.where(inside, m, owner)
            return live, next_live, owner

        live_i, _, owner_i = per_slot(i)
        live_j, next_live_j, owner_j = per_slot(j)
        ep_j = jnp.broadcast_to(episode[...].astype(jnp.float32), shape)
        ep_i = jnp.broadcast_to(
            jnp.sum(jnp.where(i == j, ep_j, 0.0), axis=1, keepdims=True), shape
        )
        keep = (j >= i) & (ep_i == ep_j) & (owner_i == owner_j)
        w_buf[...] = jnp.where(keep, live_i * live_j, 0.0)
        ep_next = jnp.broadcast_to(
            jnp.sum(jnp.where(i == j + 1, ep_i, 0.0), axis=0, keepdims=True), shape
        )
        follow = jnp.where(ep_next == ep_j, next_live_j, 0.0)
        aux[0:8, :] = live_j[0:8]
        aux[8:16, :] = follow[0:8]

    @pl.when(p == 0)
    def _():
        own_hidden.wait()
        for t in peers:
            hidden_copy(t, t).wait_recv()

    loads[0].wait()
    for t in peers:
        peer_copy(down, wd.at[t], 1, t, t).wait_recv()
    loads[1].wait()
    for t in peers:
        peer_copy(up, wu.at[t], 2, t, t).wait_recv()

    def turn():
        size = min(256, width)

        def one(b, carry):
            cs = pl.ds(pl.multiple_of(b * size, size), size)
            for f in range(n_tp):
                wd_t[f, :, cs] = wd[f, cs, :].T
                wu_t[f, cs, :] = wu[f, :, cs].T
            return carry

        lax.fori_loop(0, width // size, one, 0)

    @pl.when(p >= n_pipe // 2)
    def _():
        turn()

    def short_rows(c):
        return pl.ds(pl.multiple_of(c * CHUNK, CHUNK), CHUNK)

    def global_rows(c):
        return pl.ds(pl.multiple_of(me * own + c * CHUNK, CHUNK), CHUNK)

    def out_rows(c):
        return pl.ds(pl.multiple_of(c * fold, fold), fold)

    def fold_rows(t, c):
        return pl.ds(pl.multiple_of((t * chunks + c) * fold, fold), fold)

    def cols_of(s):
        return pl.ds(s * piece, piece)

    def forward_copy(c, s, target):
        return pltpu.make_async_remote_copy(
            src_ref=o_buf.at[out_rows(c), cols_of(s)],
            dst_ref=h_buf.at[fold_rows(me, c), cols_of(s)],
            send_sem=f_send.at[c, s],
            recv_sem=f_recv.at[c, s],
            device_id=to_pipe(target),
            device_id_type=MESH,
        )

    def backward_copy(c, s, target):
        return pltpu.make_async_remote_copy(
            src_ref=q_buf.at[out_rows(c), cols_of(s)],
            dst_ref=g_buf.at[fold_rows(me, c), cols_of(s)],
            send_sem=b_send.at[c, s],
            recv_sem=b_recv.at[c, s],
            device_id=to_pipe(target),
            device_id_type=MESH,
        )

    def grad_copy(t, c, slot):
        return pltpu.make_async_remote_copy(
            src_ref=g_buf.at[fold_rows(slot, c)],
            dst_ref=g_buf.at[fold_rows(slot, c)],
            send_sem=gx_send.at[c, t],
            recv_sem=gx_recv.at[c, slot],
            device_id=to_peer(t),
            device_id_type=MESH,
        )

    def pre_grad_copy(t, c, slot):
        rs = pl.ds(pl.multiple_of(slot * own + c * CHUNK, CHUNK), CHUNK)
        return pltpu.make_async_remote_copy(
            src_ref=pg_buf.at[rs],
            dst_ref=pg_buf.at[rs],
            send_sem=px_send.at[c, t],
            recv_sem=px_recv.at[c, slot],
            device_id=to_peer(t),
            device_id_type=MESH,
        )

    def contract(x, weight, s):
        total = jnp.zeros((CHUNK, inner), f32)
        for f in range(n_tp):
            part = jnp.dot(x, weight[f, cols_of(s), :], preferred_element_type=f32)
            total += part[f * CHUNK : (f + 1) * CHUNK]
        return total

    def expand(x, weight, s):
        return jnp.concatenate(
            [
                jnp.dot(x, weight[f, :, cols_of(s)], preferred_element_type=f32)
                for f in range(n_tp)
            ],
            axis=0,
        )

    def forward(c, carry):
        rs = fold_rows(me, c)

        @pl.when(p == 0)
        def _():
            first = c * CHUNK if sent == own else me * own + c * CHUNK
            pair = pl.ds(pl.multiple_of(first // 16 * 16, 16), 16)
            odd = lax.rem(first // CHUNK, 2) == 1
            for s in range(PIECES):
                parts = []
                for f in range(n_tp):
                    both = hid[f, pair, cols_of(s)].astype(f32)
                    parts.append(jnp.where(odd, both[CHUNK:], both[:CHUNK]))
                h_buf[rs, cols_of(s)] = jnp.concatenate(parts, axis=0).astype(bf16)

        pre = jnp.zeros((CHUNK, inner), f32)
        for s in range(PIECES):

            @pl.when(p > 0)
            def _():
                forward_copy(c, s, p - 1).wait_recv()

            pre += contract(h_buf[rs, cols_of(s)], wd, s)
        act = jax.nn.silu(pre).astype(bf16)
        for s in range(PIECES):
            out = h_buf[rs, cols_of(s)].astype(f32) + expand(act, wu, s)
            o_buf[out_rows(c), cols_of(s)] = out.astype(bf16)

            @pl.when(p < last)
            def _():
                forward_copy(c, s, p + 1).start()

        pre_buf[short_rows(c)] = pre
        act_buf[global_rows(c)] = act.astype(f32)

        @pl.when(is_last)
        def _():
            value = jnp.zeros((fold, 1), f32)
            for s in range(PIECES):
                value += jnp.sum(
                    o_buf[out_rows(c), cols_of(s)].astype(f32) * hd[:, cols_of(s)],
                    axis=1,
                    keepdims=True,
                )
            total = value[0:CHUNK]
            for f in range(1, n_tp):
                total += value[f * CHUNK : (f + 1) * CHUNK]
            vx[global_rows(c)] = jnp.broadcast_to(total, (CHUNK, vx.shape[1]))

        return carry

    @pl.when(is_last)
    def _():
        for t in peers:
            head_copy(t, t).wait_recv()

    lax.fori_loop(0, chunks, forward, 0)

    def own_rows(t):
        return pl.ds(pl.multiple_of(t * own, own), own)

    def kept_copy(t, slot):
        rs = pl.ds(pl.multiple_of(slot * chunks * fold, chunks * fold), chunks * fold)
        return peer_copy(h_buf.at[rs], h_buf.at[rs], 3, t, slot)

    def act_copy(t, slot):
        return peer_copy(act_buf.at[own_rows(slot)], act_buf.at[own_rows(slot)], 4, t, slot)

    def value_copy(t, slot):
        return peer_copy(vx.at[own_rows(slot)], vx.at[own_rows(slot)], 5, t, slot)

    @pl.when(is_last)
    def _():
        for t in peers:
            value_copy(t, me).start()
        for t in peers:
            value_copy(t, t).wait_recv()
        shape = (rows, rows)
        i = lax.broadcasted_iota(jnp.int32, shape, 0)
        j = lax.broadcasted_iota(jnp.int32, shape, 1)
        value = jnp.broadcast_to(vx[:, 0:1], shape)
        value_row = jnp.sum(jnp.where(i == j, value, 0.0), axis=0, keepdims=True)
        next_row = jnp.sum(jnp.where(i == j + 1, value, 0.0), axis=0, keepdims=True)
        delta = (rewards[...] + aux[8:9, :] * next_row - value_row) * aux[0:1, :]
        adv = jnp.sum(w_buf[...] * delta, axis=1, keepdims=True)
        adv_all = jnp.broadcast_to(adv, shape)
        w_buf[...] = adv_all
        aux[0:8, :] = jnp.broadcast_to(
            jnp.sum(jnp.where(i == j, adv_all, 0.0), axis=0, keepdims=True), (8, rows)
        )

    for t in peers:
        kept_copy(t, me).start()
        act_copy(t, me).start()

    @pl.when(p < n_pipe // 2)
    def _():
        turn()

    def signed_grad(c):
        grad = -w_buf[global_rows(c), 0:1]
        return jnp.concatenate([grad] * n_tp, axis=0)

    def backward(c, carry):
        rs = fold_rows(me, c)

        @pl.when(is_last)
        def _():
            grad = signed_grad(c)
            for s in range(PIECES):
                g_buf[rs, cols_of(s)] = (grad * hd[:, cols_of(s)]).astype(bf16)

        total = jnp.zeros((CHUNK, inner), f32)
        for s in range(PIECES):

            @pl.when(p < last)
            def _():
                backward_copy(c, s, p + 1).wait_recv()

            total += contract(g_buf[rs, cols_of(s)], wu_t, s)
        pg = (total * derivative(pre_buf[short_rows(c)])).astype(bf16)

        @pl.when(p > 0)
        def _():
            for s in range(PIECES):
                out = g_buf[rs, cols_of(s)].astype(f32) + expand(pg, wd_t, s)
                q_buf[out_rows(c), cols_of(s)] = out.astype(bf16)
                backward_copy(c, s, p - 1).start()

        pg_buf[global_rows(c)] = pg.astype(f32)
        for t in peers:
            grad_copy(t, c, me).start()
            pre_grad_copy(t, c, me).start()
        return carry

    def unfold(buf, k):
        parts = []
        for half in range(2):
            start = pl.multiple_of((2 * k + half) * fold, fold)
            both = buf[pl.ds(start, fold)].astype(f32)
            mine = both[0:CHUNK]
            for f in range(1, n_tp):
                mine = jnp.where(me == f, both[f * CHUNK : (f + 1) * CHUNK], mine)
            parts.append(mine)
        return jnp.concatenate(parts, axis=0).astype(bf16)

    def flat_pass(buf, index):
        def one(k, carry):
            flat[index, pl.ds(pl.multiple_of(k * 16, 16), 16)] = unfold(buf, k)
            return carry

        lax.fori_loop(0, rows // 16, one, 0)

    def keep():
        for t in peers:
            kept_copy(t, t).wait_recv()
            act_copy(t, t).wait_recv()
        flat_pass(h_buf, 0)
        narrow[0] = act_buf[...].astype(bf16)
        copies[0].start()
        copies[1].start()

    copies = [
        pltpu.make_async_copy(flat.at[0], h_out, local_sem.at[0]),
        pltpu.make_async_copy(narrow.at[0], act_out, local_sem.at[1]),
        pltpu.make_async_copy(flat.at[1], g_out, local_sem.at[2]),
        pltpu.make_async_copy(narrow.at[1], pg_out, local_sem.at[3]),
    ]

    @pl.when(p < last)
    def _():
        keep()

    lax.fori_loop(0, chunks, backward, 0)

    @pl.when(is_last)
    def _():
        keep()

    def gather(c, carry):
        for t in peers:
            grad_copy(t, c, t).wait_recv()
            pre_grad_copy(t, c, t).wait_recv()
        return carry

    lax.fori_loop(0, chunks, gather, 0)
    flat_pass(g_buf, 1)
    narrow[1] = pg_buf[...].astype(bf16)
    copies[2].start()
    copies[3].start()

    slice_width = width // n_pipe

    def message_copy(q):
        return pltpu.make_async_remote_copy(
            src_ref=msg.at[q],
            dst_ref=msg_in,
            send_sem=msg_send.at[q],
            recv_sem=msg_recv.at[0],
            device_id=to_pipe(q),
            device_id_type=MESH,
        )

    def head_rows(t):
        return pl.ds(pl.multiple_of(t * CHUNK, CHUNK), CHUNK)

    def head_grad_copy(t, slot):
        return peer_copy(o_sum.at[head_rows(t)], ghx.at[slot], 7, t, slot)

    @pl.when(is_last)
    def _():
        for s in range(PIECES):
            acc = jnp.zeros((fold, piece), f32)
            for c in range(chunks):
                acc += o_buf[out_rows(c), cols_of(s)].astype(f32) * signed_grad(c)
            o_sum[:, cols_of(s)] = acc
        ghx[me] = o_sum[head_rows(me)]
        for t in peers:
            head_grad_copy(t, me).start()
        for t in peers:
            head_grad_copy(t, t).wait_recv()
        adv_row = aux[0:1, :]
        for b in range(width // block):
            cs = pl.ds(b * block, block)
            acc = ghx[0, :, cs]
            for t in range(1, n_tp):
                acc += ghx[t, :, cs]
            head_grad = jnp.sum(acc, axis=0, keepdims=True)
            for q in range(n_pipe):
                if q * slice_width // block == b:
                    msg[q, 0:1, :] = head_grad
                    msg[q, 1:2, 0:rows] = adv_row
        for q in range(last):
            message_copy(q).start()
        msg_out[...] = msg[last]

    @pl.when(p < last)
    def _():
        message_copy(last).wait_recv()
        msg_out[...] = msg_in[...]

    def finish(c, carry):
        for s in range(PIECES):

            @pl.when(p < last)
            def _():
                forward_copy(c, s, p + 1).wait_send()

            @pl.when(p > 0)
            def _():
                backward_copy(c, s, p - 1).wait_send()

        for t in peers:
            grad_copy(t, c, me).wait_send()
            pre_grad_copy(t, c, me).wait_send()
        return carry

    lax.fori_loop(0, chunks, finish, 0)

    @pl.when(p == 0)
    def _():
        for t in peers:
            hidden_copy(t, me).wait_send()

    for t in peers:
        peer_copy(down, wd.at[me], 1, t, me).wait_send()
        peer_copy(up, wu.at[me], 2, t, me).wait_send()
        kept_copy(t, me).wait_send()
        act_copy(t, me).wait_send()

    @pl.when(is_last)
    def _():
        for t in peers:
            head_copy(t, me).wait_send()
            value_copy(t, me).wait_send()
            head_grad_copy(t, me).wait_send()
        for q in range(last):
            message_copy(q).wait_send()

    for copy in copies:
        copy.wait()


def local(hidden, rewards, counts, episode, down_weight, up_weight, head_weight):
    n_pipe = lax.axis_size("pipe")
    n_tp = lax.axis_size("tp")
    batch, cap, width = hidden.shape
    rows = batch * cap
    down, up = down_weight[0], up_weight[0]
    inner = down.shape[1]
    own = rows // n_tp
    sent = own if own % 16 == 0 else rows
    chunks = own // CHUNK
    slice_width = width // n_pipe
    block = max(slice_width, 128)
    bf16, f32 = jnp.bfloat16, jnp.float32
    vmem = pl.BlockSpec(memory_space=pltpu.VMEM)
    smem = pl.BlockSpec(memory_space=pltpu.SMEM)
    anywhere = pl.BlockSpec(memory_space=pl.ANY)
    dma = pltpu.SemaphoreType.DMA
    h, act, pg, g, msg = pl.pallas_call(
        functools.partial(kernel, n_pipe, n_tp, batch),
        out_shape=(
            jax.ShapeDtypeStruct((rows, width), bf16),
            jax.ShapeDtypeStruct((rows, inner), bf16),
            jax.ShapeDtypeStruct((rows, inner), bf16),
            jax.ShapeDtypeStruct((rows, width), bf16),
            jax.ShapeDtypeStruct((8, block), f32),
        ),
        in_specs=[anywhere, vmem, smem, vmem, anywhere, anywhere, vmem],
        out_specs=(anywhere, anywhere, anywhere, anywhere, vmem),
        scratch_shapes=[
            pltpu.VMEM((n_tp, sent, width), bf16),
            pltpu.VMEM((n_tp * rows, width), bf16),
            pltpu.VMEM((rows, width), bf16),
            pltpu.VMEM((n_tp * rows, width), bf16),
            pltpu.VMEM((rows, width), bf16),
            pltpu.VMEM((2, rows, width), bf16),
            pltpu.VMEM((2, rows, inner), bf16),
            pltpu.VMEM((rows, inner), f32),
            pltpu.VMEM((rows, inner), f32),
            pltpu.VMEM((own, inner), f32),
            pltpu.VMEM((n_tp, width, inner), bf16),
            pltpu.VMEM((n_tp, inner, width), bf16),
            pltpu.VMEM((n_tp, inner, width), bf16),
            pltpu.VMEM((n_tp, width, inner), bf16),
            pltpu.VMEM((n_tp * CHUNK, width), f32),
            pltpu.VMEM((n_tp * CHUNK, width), f32),
            pltpu.VMEM((n_tp, CHUNK, width), f32),
            pltpu.VMEM((rows, 128), f32),
            pltpu.VMEM((rows, rows), f32),
            pltpu.VMEM((16, rows), f32),
            pltpu.VMEM((n_pipe, 8, block), f32),
            pltpu.VMEM((8, block), f32),
            dma((chunks, PIECES)),
            dma((chunks, PIECES)),
            dma((chunks, PIECES)),
            dma((chunks, PIECES)),
            dma((chunks, n_tp)),
            dma((chunks, n_tp)),
            dma((chunks, n_tp)),
            dma((chunks, n_tp)),
            dma((8, n_tp)),
            dma((8, n_tp)),
            dma((n_pipe,)),
            dma((1,)),
            dma((4,)),
        ],
        compiler_params=pltpu.CompilerParams(
            collective_id=0, has_side_effects=True, vmem_limit_bytes=56 * 1024 * 1024
        ),
        name="adapters",
    )(
        hidden.reshape(rows, width),
        rewards.reshape(1, rows),
        counts,
        episode.reshape(1, rows),
        down,
        up,
        head_weight.reshape(1, width),
    )
    grad_down = jnp.einsum("nd,nk->dk", h, pg, preferred_element_type=f32)
    grad_up = jnp.einsum("nk,nd->kd", act, g, preferred_element_type=f32)
    offset = lax.rem(lax.axis_index("pipe") * slice_width, block)
    grad_head = lax.dynamic_slice(msg, (0, offset), (1, slice_width))
    advantages = msg[1, :rows].reshape(batch, cap)
    return (grad_down[None], grad_up[None], grad_head[None].reshape(1, slice_width), advantages)


def solution(mesh):
    return jax.shard_map(
        local,
        mesh=mesh,
        in_specs=(
            P(None, None, "tp"),
            P(),
            P(),
            P(),
            P("pipe", "tp", None),
            P("pipe", None, "tp"),
            P("tp"),
        ),
        out_specs=(P("pipe", "tp", None), P("pipe", None, "tp"), P("tp", "pipe"), P()),
        check_vma=False,
    )
```

time: 276 us -> 236 us (0.86)
  Pallas kernels: 261 us -> 222 us
    pallas_call x1, Pallas kernels: 261 us -> 222 us  [local(): pl.pallas_call(functools.partial(kernel, n_pipe, n_tp, batch), out_shape=...]
    unnamed x8 -> x4, local copies, waits for them, and re-layouts: 5.06 us -> 0.01 us
where the time goes in v2:
time: 236 us
  Pallas kernels  222 us (94%)
  matrix products  6.71 us (3%)
  local copies, waits for them, and re-layouts  6.55 us (3%)
    pallas_call x1, Pallas kernels, local(): pl.pallas_call(functools.partial(kernel, n_pipe, n_tp, batch), out_shape=...  222 us

profile of v2, /device:TPU:1, one launch (start us, length us, event | category | flops | bytes accessed | tf_op | source)
XLA Modules:
  0.0 235.8 jit_solution(9101856495391951301)
XLA Ops:
  0.6 1.3 reshape.21.rewards
  1.9 1.3 reshape.22.episode
  3.2 1.3 reshape.23.head
  4.5 221.9 %adapters.1 = (bf16[128,4096]{1,0:T(8,128)(2,1)}, bf16[128,256]{1,0:T(8,128)(2,1)}, bf16[128,256]{1,0:T(8,128)(2,1)}, bf16[128,4096]{1,0:T(8,128)(2,1)}, f32[8,256]{1,0:T(8,128)}) custom-call(bf16[128,4096]{1,0:T(8,128)(2,1)} %bitcast.13, f32[1,128]{1,0:T(1,128)} %reshape.21.rewards, s32[2]{0:T(128)} %counts.1, s32[1,128]{1,0:T(1,128)} %reshape.22.episode, ...), custom_call_target="tpu_custom_call" | custom-call | tf_op jit(solution)/shard_map/adapters/pallas_call | solution.py:611
  226.3 0.0 copy-start
  226.4 0.0 copy-start.1
  226.4 0.8 slice_reduce_fusion
  227.2 1.3 dynamic_slice.4
  228.4 0.6 reshape_squeeze.3
  229.1 4.0 %convolution_bitcast_fusion.1 = f32[1,4096,256]{2,1,0:T(8,128)} fusion(bf16[128,4096]{1,0:T(8,128)(2,1)} %get-tuple-element.9, bf16[128,256]{1,0:T(8,128)(2,1)} %get-tuple-element.10), kind=kOutput, calls=%fused_computation.1 | convolution fusion | flops 268435456 | bytes 5308416 | tf_op jit(solution)/shard_map/nd,nk->dk/dot_general | solution.py:672
  233.0 0.0 copy-done
  233.0 0.0 copy-done.1
  233.0 2.7 %convolution_bitcast_fusion = f32[1,256,4096]{2,1,0:T(8,128)} fusion(bf16[128,256]{1,0:T(8,128)(2,1)S(1)} %copy-done.1, bf16[128,4096]{1,0:T(8,128)(2,1)S(1)} %copy-done), kind=kOutput, calls=%fused_computation | convolution fusion | flops 268435456 | bytes 5308416 | tf_op jit(solution)/shard_map/nk,nd->kd/dot_general | solution.py:673
Async XLA Ops:
  226.3 6.7 %copy-start = (bf16[128,4096]{1,0:T(8,128)(2,1)S(1)}, bf16[128,4096]{1,0:T(8,128)(2,1)}, u32[]{:S(2)}) copy-start(bf16[128,4096]{1,0:T(8,128)(2,1)} %get-tuple-element.12) | copy-start | bytes 3145732
  226.4 6.7 %copy-start.1 = (bf16[128,256]{1,0:T(8,128)(2,1)S(1)}, bf16[128,256]{1,0:T(8,128)(2,1)}, u32[]{:S(2)}) copy-start(bf16[128,256]{1,0:T(8,128)(2,1)} %get-tuple-element.11) | copy-start | bytes 196612

commit v3 on v2

--- a/solution.py
+++ b/solution.py
@@ -168,7 +168,7 @@
     @pl.when(is_last)
     def _():
         hd[pl.ds(pl.multiple_of(me * CHUNK, CHUNK), CHUNK), :] = jnp.broadcast_to(
-            head[...].astype(f32), (CHUNK, width)
+            head[...].astype(f32).reshape(1, width), (CHUNK, width)
         )
         for t in peers:
             head_copy(t, me).start()
@@ -179,6 +179,9 @@
         i = lax.broadcasted_iota(jnp.int32, shape, 0)
         j = lax.broadcasted_iota(jnp.int32, shape, 1)
         cap = rows // batch
+        for m in range(batch):
+            aux[16:17, m * cap : (m + 1) * cap] = rewards[m : m + 1, :]
+            aux[24:25, m * cap : (m + 1) * cap] = episode[m : m + 1, :].astype(f32)
 
         def per_slot(idx):
             live = jnp.zeros(shape, jnp.float32)
@@ -194,7 +197,7 @@
 
         live_i, _, owner_i = per_slot(i)
         live_j, next_live_j, owner_j = per_slot(j)
-        ep_j = jnp.broadcast_to(episode[...].astype(jnp.float32), shape)
+        ep_j = jnp.broadcast_to(aux[24:25, :], shape)
         ep_i = jnp.broadcast_to(
             jnp.sum(jnp.where(i == j, ep_j, 0.0), axis=1, keepdims=True), shape
         )
@@ -308,11 +311,10 @@
             axis=0,
         )
 
-    def forward(c, carry):
+    def forward(first_layer, final_layer, c, carry):
         rs = fold_rows(me, c)
 
-        @pl.when(p == 0)
-        def _():
+        if first_layer:
             first = c * CHUNK if sent == own else me * own + c * CHUNK
             pair = pl.ds(pl.multiple_of(first // 16 * 16, 16), 16)
             odd = lax.rem(first // CHUNK, 2) == 1
@@ -326,8 +328,7 @@
         pre = jnp.zeros((CHUNK, inner), f32)
         for s in range(PIECES):
 
-            @pl.when(p > 0)
-            def _():
+            if not first_layer:
                 forward_copy(c, s, p - 1).wait_recv()
 
             pre += contract(h_buf[rs, cols_of(s)], wd, s)
@@ -336,15 +337,13 @@
             out = h_buf[rs, cols_of(s)].astype(f32) + expand(act, wu, s)
             o_buf[out_rows(c), cols_of(s)] = out.astype(bf16)
 
-            @pl.when(p < last)
-            def _():
+            if not final_layer:
                 forward_copy(c, s, p + 1).start()
 
         pre_buf[short_rows(c)] = pre
         act_buf[global_rows(c)] = act.astype(f32)
 
-        @pl.when(is_last)
-        def _():
+        if final_layer:
             value = jnp.zeros((fold, 1), f32)
             for s in range(PIECES):
                 value += jnp.sum(
@@ -359,12 +358,25 @@
 
         return carry
 
+    def by_place(body):
+        @pl.when(p == 0)
+        def _():
+            lax.fori_loop(0, chunks, functools.partial(body, True, n_pipe == 1), 0)
+
+        @pl.when((p > 0) & (p < last))
+        def _():
+            lax.fori_loop(0, chunks, functools.partial(body, False, False), 0)
+
+        @pl.when((p > 0) & is_last)
+        def _():
+            lax.fori_loop(0, chunks, functools.partial(body, False, True), 0)
+
     @pl.when(is_last)
     def _():
         for t in peers:
             head_copy(t, t).wait_recv()
 
-    lax.fori_loop(0, chunks, forward, 0)
+    by_place(forward)
 
     def own_rows(t):
         return pl.ds(pl.multiple_of(t * own, own), own)
@@ -391,7 +403,7 @@
         value = jnp.broadcast_to(vx[:, 0:1], shape)
         value_row = jnp.sum(jnp.where(i == j, value, 0.0), axis=0, keepdims=True)
         next_row = jnp.sum(jnp.where(i == j + 1, value, 0.0), axis=0, keepdims=True)
-        delta = (rewards[...] + aux[8:9, :] * next_row - value_row) * aux[0:1, :]
+        delta = (aux[16:17, :] + aux[8:9, :] * next_row - value_row) * aux[0:1, :]
         adv = jnp.sum(w_buf[...] * delta, axis=1, keepdims=True)
         adv_all = jnp.broadcast_to(adv, shape)
         w_buf[...] = adv_all
@@ -411,11 +423,10 @@
         grad = -w_buf[global_rows(c), 0:1]
         return jnp.concatenate([grad] * n_tp, axis=0)
 
-    def backward(c, carry):
+    def backward(first_layer, final_layer, c, carry):
         rs = fold_rows(me, c)
 
-        @pl.when(is_last)
-        def _():
+        if final_layer:
             grad = signed_grad(c)
             for s in range(PIECES):
                 g_buf[rs, cols_of(s)] = (grad * hd[:, cols_of(s)]).astype(bf16)
@@ -423,15 +434,13 @@
         total = jnp.zeros((CHUNK, inner), f32)
         for s in range(PIECES):
 
-            @pl.when(p < last)
-            def _():
+            if not final_layer:
                 backward_copy(c, s, p + 1).wait_recv()
 
             total += contract(g_buf[rs, cols_of(s)], wu_t, s)
         pg = (total * derivative(pre_buf[short_rows(c)])).astype(bf16)
 
-        @pl.when(p > 0)
-        def _():
+        if not first_layer:
             for s in range(PIECES):
                 out = g_buf[rs, cols_of(s)].astype(f32) + expand(pg, wd_t, s)
                 q_buf[out_rows(c), cols_of(s)] = out.astype(bf16)
@@ -481,7 +490,7 @@
     def _():
         keep()
 
-    lax.fori_loop(0, chunks, backward, 0)
+    by_place(backward)
 
     @pl.when(is_last)
     def _():
@@ -589,6 +598,18 @@
 
     for copy in copies:
         copy.wait()
+
+
+def gradients(h, act, pg, g, msg, grad_down, grad_up, head_row, advantages):
+    over_rows = (((0,), (0,)), ((), ()))
+    grad_down[...] = lax.dot_general(
+        h[...], pg[...], over_rows, preferred_element_type=jnp.float32
+    )
+    grad_up[...] = lax.dot_general(act[...], g[...], over_rows, preferred_element_type=jnp.float32)
+    head_row[...] = msg[0:1, :]
+    batch, cap = advantages.shape
+    for m in range(batch):
+        advantages[m : m + 1, :] = msg[1:2, m * cap : (m + 1) * cap]
 
 
 def local(hidden, rewards, counts, episode, down_weight, up_weight, head_weight):
@@ -639,7 +660,7 @@
             pltpu.VMEM((n_tp, CHUNK, width), f32),
             pltpu.VMEM((rows, 128), f32),
             pltpu.VMEM((rows, rows), f32),
-            pltpu.VMEM((16, rows), f32),
+            pltpu.VMEM((32, rows), f32),
             pltpu.VMEM((n_pipe, 8, block), f32),
             pltpu.VMEM((8, block), f32),
             dma((chunks, PIECES)),
@@ -662,19 +683,48 @@
         name="adapters",
     )(
         hidden.reshape(rows, width),
-        rewards.reshape(1, rows),
+        rewards,
         counts,
-        episode.reshape(1, rows),
+        episode,
         down,
         up,
-        head_weight.reshape(1, width),
+        head_weight,
     )
-    grad_down = jnp.einsum("nd,nk->dk", h, pg, preferred_element_type=f32)
-    grad_up = jnp.einsum("nk,nd->kd", act, g, preferred_element_type=f32)
-    offset = lax.rem(lax.axis_index("pipe") * slice_width, block)
-    grad_head = lax.dynamic_slice(msg, (0, offset), (1, slice_width))
-    advantages = msg[1, :rows].reshape(batch, cap)
-    return (grad_down[None], grad_up[None], grad_head[None].reshape(1, slice_width), advantages)
+    tile = min(512, width)
+    exact = slice_width == block
+
+    def whole(shape):
+        return pl.BlockSpec(shape, lambda b: (0, 0))
+
+    grad_down, grad_up, head_row, advantages = pl.pallas_call(
+        gradients,
+        grid=(width // tile,),
+        out_shape=(
+            jax.ShapeDtypeStruct((width, inner), f32),
+            jax.ShapeDtypeStruct((inner, width), f32),
+            jax.ShapeDtypeStruct((1, block), f32),
+            jax.ShapeDtypeStruct((batch, cap), f32),
+        ),
+        in_specs=[
+            pl.BlockSpec((rows, tile), lambda b: (0, b)),
+            whole((rows, inner)),
+            whole((rows, inner)),
+            pl.BlockSpec((rows, tile), lambda b: (0, b)),
+            whole((8, block)),
+        ],
+        out_specs=(
+            pl.BlockSpec((tile, inner), lambda b: (b, 0)),
+            pl.BlockSpec((inner, tile), lambda b: (0, b)),
+            whole((1, block)),
+            whole((batch, cap)),
+        ),
+        compiler_params=pltpu.CompilerParams(vmem_limit_bytes=60 * 1024 * 1024),
+        name="gradients",
+    )(h, act, pg, g, msg)
+    if not exact:
+        offset = lax.rem(lax.axis_index("pipe") * slice_width, block)
+        head_row = lax.dynamic_slice(head_row, (0, offset), (1, slice_width))
+    return (grad_down[None], grad_up[None], head_row, advantages)
 
 
 def solution(mesh):

time: 236 us -> 229 us (0.970)
  matrix products: 6.71 us -> 0 us
  local copies, waits for them, and re-layouts: 6.55 us -> 0 us
  Pallas kernels: 222 us -> 228 us
    pallas_call x0 -> x1, Pallas kernels: none -> 7.99 us  [local(): pl.pallas_call(gradients, grid=(width // tile,), out_shape=(jax.ShapeDtyp...]
    dot_general x2 -> x0, matrix products: 6.71 us -> none  [the longest x1 3.97 us: local(): grad_down = jnp.einsum('nd,nk->dk', h, pg, preferred_element_type=f32)]
    reshape x3 -> x0, local copies, waits for them, and re-layouts: 3.85 us -> none  [the longest x1 1.31 us: local(): head_weight.reshape(1, width)]
where the time goes in v3:
time: 229 us
  Pallas kernels  228 us (100%)
    pallas_call x1, Pallas kernels, local(): pl.pallas_call(functools.partial(kernel, n_pipe, n_tp, batch), out_shape=...  220 us
    pallas_call x1, Pallas kernels, local(): pl.pallas_call(gradients, grid=(width // tile,), out_shape=(jax.ShapeDtyp...  7.99 us

profile of v3, /device:TPU:1, one launch (start us, length us, event | category | flops | bytes accessed | tf_op | source)
XLA Modules:
  0.0 228.5 jit_solution(1518344577669129116)
XLA Ops:
  0.6 219.9 %adapters.1 = (bf16[128,4096]{1,0:T(8,128)(2,1)}, bf16[128,256]{1,0:T(8,128)(2,1)}, bf16[128,256]{1,0:T(8,128)(2,1)}, bf16[128,4096]{1,0:T(8,128)(2,1)}, f32[8,256]{1,0:T(8,128)}) custom-call(bf16[128,4096]{1,0:T(8,128)(2,1)} %bitcast.7, f32[2,64]{1,0:T(2,128)} %rewards.1, s32[2]{0:T(128)} %counts.1, s32[2,64]{1,0:T(2,128)} %episode.1, ...), custom_call_target="tpu_custom_call" | custom-call | tf_op jit(solution)/shard_map/adapters/pallas_call | solution.py:632
  220.6 8.0 %gradients.1 = (f32[4096,256]{1,0:T(8,128)}, f32[256,4096]{1,0:T(8,128)}, f32[1,256]{1,0:T(1,128)}, f32[2,64]{1,0:T(2,128)}) custom-call(bf16[128,4096]{1,0:T(8,128)(2,1)} %get-tuple-element.13.h, bf16[128,256]{1,0:T(8,128)(2,1)} %get-tuple-element.14.act, bf16[128,256]{1,0:T(8,128)(2,1)} %get-tuple-element.15.pg, bf16[128,4096]{1,0:T(8,128)(2,1)} %get-tuple-element.16.g, ...), custom_call_target="tpu_custom_call" | custom-call | tf_op jit(solution)/shard_map/gradients/pallas_call | solution.py:699

commit v4 on v3

--- a/solution.py
+++ b/solution.py
@@ -690,7 +690,7 @@
         up,
         head_weight,
     )
-    tile = min(512, width)
+    tile = min(1024, width)
     exact = slice_width == block
 
     def whole(shape):

time: 229 us -> 227 us (level)
  no operation moved by 1% of the time
where the time goes in v4:
time: 227 us; the launch traced here: 226 us
  Pallas kernels  226 us (100%)
    pallas_call x1, Pallas kernels, local(): pl.pallas_call(functools.partial(kernel, n_pipe, n_tp, batch), out_shape=...  220 us
    pallas_call x1, Pallas kernels, local(): pl.pallas_call(gradients, grid=(width // tile,), out_shape=(jax.ShapeDtyp...  5.94 us

profile of v4, /device:TPU:1, one launch (start us, length us, event | category | flops | bytes accessed | tf_op | source)
XLA Modules:
  0.0 226.5 jit_solution(17835892437980219567)
XLA Ops:
  0.6 219.9 %adapters.1 = (bf16[128,4096]{1,0:T(8,128)(2,1)}, bf16[128,256]{1,0:T(8,128)(2,1)}, bf16[128,256]{1,0:T(8,128)(2,1)}, bf16[128,4096]{1,0:T(8,128)(2,1)}, f32[8,256]{1,0:T(8,128)}) custom-call(bf16[128,4096]{1,0:T(8,128)(2,1)} %bitcast.7, f32[2,64]{1,0:T(2,128)} %rewards.1, s32[2]{0:T(128)} %counts.1, s32[2,64]{1,0:T(2,128)} %episode.1, ...), custom_call_target="tpu_custom_call" | custom-call | tf_op jit(solution)/shard_map/adapters/pallas_call | solution.py:632
  220.6 5.9 %gradients.1 = (f32[4096,256]{1,0:T(8,128)}, f32[256,4096]{1,0:T(8,128)}, f32[1,256]{1,0:T(1,128)}, f32[2,64]{1,0:T(2,128)}) custom-call(bf16[128,4096]{1,0:T(8,128)(2,1)} %get-tuple-element.13.h, bf16[128,256]{1,0:T(8,128)(2,1)} %get-tuple-element.14.act, bf16[128,256]{1,0:T(8,128)(2,1)} %get-tuple-element.15.pg, bf16[128,4096]{1,0:T(8,128)(2,1)} %get-tuple-element.16.g, ...), custom_call_target="tpu_custom_call" | custom-call | tf_op jit(solution)/shard_map/gradients/pallas_call | solution.py:699
